TPU v7x, 32 devices: a whole 2x2x4 slice. The times are simulated.
32 devices in a mesh: dp: 8 (over z, core), ctx: 4 (over y, x).
Axes of the slice: x: 2, y: 2, z: 4, core: 2. Of those that a mesh axis runs over, the one named last changes fastest.
Arguments:
- layer_input: bfloat16 [8, 512, 8192], P('dp', 'ctx'), may hold values from -6 to 6
- queries: bfloat16 [8, 512, 1024], P('dp', 'ctx'), may hold values from -68 to 68
- key_rows: bfloat16 [8, 512, 128], P('dp', 'ctx'), may hold values from -4 to 4
- value_rows: bfloat16 [8, 512, 128], P('dp', 'ctx'), may hold values from -5 to 5
- grad_output: bfloat16 [8, 512, 1024], P('dp', 'ctx'), may hold values from -12 to 12
- segments: int32 [8, 512], P('dp'), may hold values from 0 to 2, never falling along the last dimension, each value on 1 to 256 neighbouring positions
- lengths: int32 [8], P('dp'), may hold values from 256 to 512, as said below
Outputs:
- grad_queries: bfloat16 [8, 512, 1024], P('dp', 'ctx')
- grad_weights: bfloat16 [8192, 256], P(('dp', 'ctx'))
Inputs may be any that keep to these rules, and one draw needn't show every extreme that they name: `lengths`: some rollout has all 512 positions live.
All inputs are finite; a program needn't handle non-finite values.
Results may differ from a plain program's by a relative error of at most 0.0057.
Values may be sent and summed in bfloat16 or wider, within the bound.
A program may use at most 64 MiB of HBM per device.

v0:
```python
import math

import jax
import jax.numpy as jnp
from jax import lax
from jax.sharding import PartitionSpec as P


def passed_along(x, axis, by):
    length = lax.axis_size(axis)
    pairs = [(i, i + by) for i in range(length) if 0 <= i + by < length]
    return lax.ppermute(x, axis, pairs)


def make_mask(query_seg, key_seg, query_pos, key_pos, length, window_len):
    gap = query_pos[:, None] - key_pos[None, :]
    same_doc = query_seg[:, None] == key_seg[None, :]
    inside = (gap >= 0) & (gap < window_len)
    alive = (key_pos[None, :] < length) | (gap == 0)
    return same_doc & inside & alive


def block_grads(query_blk, upstream, key_all, allowed, live, score_scale):
    head_size = key_all.shape[1] // 2
    key_part = key_all[:, :head_size]
    value_part = key_all[:, head_size:]
    scores = (
        jnp.einsum("rgd,kd->grk", query_blk, key_part, preferred_element_type=jnp.float32)
        * score_scale
    )
    masked = jnp.where(allowed[None], scores, -1e30)
    row_max = jnp.max(masked, axis=2, keepdims=True)
    unnorm = jnp.where(allowed[None], jnp.exp(masked - row_max), 0.0)
    probs = unnorm / jnp.sum(unnorm, axis=2, keepdims=True) * live[None, :, None]
    probs_low = probs.astype(jnp.bfloat16)
    dprobs = jnp.einsum("rgd,kd->grk", upstream, value_part, preferred_element_type=jnp.float32)
    row_dot = jnp.sum(probs * dprobs, axis=2, keepdims=True)
    dscores = (probs * (dprobs - row_dot)).astype(jnp.bfloat16)
    grad_q = (
        jnp.einsum("grk,kd->rgd", dscores, key_part, preferred_element_type=jnp.float32)
        * score_scale
    ).astype(jnp.bfloat16)
    grad_k = (
        jnp.einsum("grk,rgd->kd", dscores, query_blk, preferred_element_type=jnp.float32)
        * score_scale
    )
    grad_v = jnp.einsum("grk,rgd->kd", probs_low, upstream, preferred_element_type=jnp.float32)
    return (grad_q.reshape(query_blk.shape[0], -1), jnp.concatenate([grad_k, grad_v], axis=1))


def shards(layer_input, queries, key_rows, value_rows, grad_output, segments, lengths):
    ctx_count = lax.axis_size("ctx")
    dp_count = lax.axis_size("dp")
    ctx_place = lax.axis_index("ctx")
    row_count = layer_input.shape[1]
    width_all = layer_input.shape[2]
    head_size = key_rows.shape[2]
    group_size = queries.shape[2] // head_size
    reach_count = min(8, ctx_count // 2)
    window_len = reach_count * row_count
    score_scale = 1.0 / math.sqrt(head_size)
    local_pair = jnp.concatenate([key_rows[0], value_rows[0]], axis=1)
    earlier = []
    for offset in range(1, reach_count + 1):
        earlier.append(passed_along(local_pair, "ctx", offset))
    key_all = jnp.concatenate(earlier[::-1] + [local_pair], axis=0)
    length = lengths[0]
    seg_row = segments[0]
    seg_pad = jnp.concatenate([jnp.full((window_len,), -1, jnp.int32), seg_row])
    first_row = ctx_place * row_count
    query_seg = lax.dynamic_slice_in_dim(seg_row, first_row, row_count, 0)
    key_seg = lax.dynamic_slice_in_dim(seg_pad, first_row, window_len + row_count, 0)
    query_pos = first_row + jnp.arange(row_count, dtype=jnp.int32)
    key_pos = first_row - window_len + jnp.arange(window_len + row_count, dtype=jnp.int32)
    allowed = make_mask(query_seg, key_seg, query_pos, key_pos, length, window_len)
    live = (query_pos < length).astype(jnp.float32)
    query_blk = queries[0].reshape(row_count, group_size, head_size)
    upstream = grad_output[0].reshape(row_count, group_size, head_size)
    grad_q, contrib = block_grads(query_blk, upstream, key_all, allowed, live, score_scale)
    blocks = contrib.reshape(reach_count + 1, row_count, 2 * head_size)
    total = blocks[reach_count]
    for offset in range(1, reach_count + 1):
        total = total + passed_along(blocks[reach_count - offset], "ctx", -offset)
    grad_kv = total.astype(jnp.bfloat16)
    slab_rows = width_all // (dp_count * ctx_count)
    inputs_flat = layer_input[0]
    partial_value = jnp.einsum(
        "rd,rc->dc", inputs_flat, grad_kv, preferred_element_type=jnp.float32
    )
    pieces = partial_value.reshape(dp_count, ctx_count, slab_rows, 2 * head_size)
    moved = lax.all_to_all(pieces, "ctx", split_axis=1, concat_axis=1, tiled=True)
    rollout_part = jnp.sum(moved, axis=1).reshape(dp_count * slab_rows, 2 * head_size)
    summed = lax.psum_scatter(rollout_part, "dp", scatter_dimension=0, tiled=True)
    grad_weights = (summed / dp_count).astype(jnp.bfloat16)
    return (grad_q.reshape(1, row_count, group_size * head_size), grad_weights)


def solution(mesh):
    return jax.shard_map(
        shards,
        mesh=mesh,
        in_specs=(
            P("dp", "ctx", None),
            P("dp", "ctx", None),
            P("dp", "ctx", None),
            P("dp", "ctx", None),
            P("dp", "ctx", None),
            P("dp", None),
            P("dp"),
        ),
        out_specs=(P("dp", "ctx", None), P(("dp", "ctx"), None)),
        check_vma=False,
    )
```

profile of v0, /device:TPU:0, one launch (start us, length us, event | category | flops | bytes accessed | tf_op | source)
XLA Modules:
  0.0 203.4 jit_solution(1182520907572265989)
XLA Ops:
  7.2 0.0 copy-start
  7.2 0.0 reduce-scatter.2.cloned.1.call-start
  7.2 0.9 pad_maximum_fusion.1
  8.1 4.8 %collective-permute-start.1 = (bf16[128,256]{1,0:T(8,128)(2,1)S(1)}, bf16[128,256]{1,0:T(8,128)(2,1)S(1)}, u32[]{:S(2)}, u32[]{:S(2)}) collective-permute-start(bf16[128,256]{1,0:T(8,128)(2,1)S(1)} %pad_maximum_fusion.1), channel_id=1, source_target_pairs={{0,1},{1,2},{2,3},{4,5},{5,6},{6,7},{8,9},{9,10},{10,11},{12,13},{... | collective-permute-start | bytes 196616 | tf_op jit(solution)/shard_map/ppermute | solution.py:12
  13.0 3.4 %collective-permute-start = (bf16[128,256]{1,0:T(8,128)(2,1)S(1)}, bf16[128,256]{1,0:T(8,128)(2,1)S(1)}, u32[]{:S(2)}, u32[]{:S(2)}) collective-permute-start(bf16[128,256]{1,0:T(8,128)(2,1)S(1)} %pad_maximum_fusion.1), channel_id=1, source_target_pairs={{0,2},{1,3},{4,6},{5,7},{8,10},{9,11},{12,14},{13,15},{16,18},{17,... | collective-permute-start | bytes 196616 | tf_op jit(solution)/shard_map/ppermute | solution.py:12
  17.1 1.1 copy.37
  18.2 1.1 copy.38
  19.4 0.7 dynamic-slice_bitcast_fusion
  20.0 0.8 pad_dynamic-slice_fusion
  20.8 0.2 fusion.11
  21.0 0.0 collective-permute-done.1
  21.0 0.0 collective-permute-done
  21.0 0.8 maximum_maximum_fusion
  21.8 1.8 fusion.24
  23.7 0.0 copy-start.1
  23.7 1.9 convolution_bitcast_fusion.1
  25.6 0.0 copy-done.1
  25.6 0.4 fusion.3
  26.0 0.3 fusion.5
  26.3 0.4 fusion.7
  26.7 1.3 collective-permute-start.2
  28.0 1.3 collective-permute-start.3
  29.3 4.3 %collective-permute-done.2 = f32[128,256]{0,1:T(8,128)S(1)} collective-permute-done((f32[128,256]{0,1:T(8,128)S(1)}, f32[128,256]{0,1:T(8,128)S(1)}, u32[]{:S(2)}, u32[]{:S(2)}) %collective-permute-start.2) | collective-permute-done | bytes 131104 | tf_op jit(solution)/shard_map/ppermute | solution.py:12
  33.5 1.3 collective-permute-done.3
  34.8 0.0 copy-done
  34.8 4.5 %convolution_bitcast_fusion = f32[8192,256]{0,1:T(8,128)} fusion(bf16[1,128,8192]{2,1,0:T(8,128)(2,1)S(1)} %copy-done, f32[128,256]{0,1:T(8,128)S(1)} %collective-permute-done.3, f32[128,256]{0,1:T(8,128)S(1)} %collective-permute-done.2, f32[384,128]{0,1:T(8,128)S(1)} %fusion.7, f32[384,128]{0,1:T(8,128)S(1)} %convolution_bitcast_fusion.1), kind=kOutput, calls=%fused_computation.1 | convolution fusion | flops 537001984 | bytes 11141120 | tf_op jit(solution)/shard_map/rd,rc->dc/dot_general | solution.py:87
  39.3 10.8 %reshape.117 = f32[8,4,256,256]{2,1,0,3:T(4,128)} reshape(f32[8192,256]{0,1:T(8,128)} %convolution_bitcast_fusion) | data formatting | bytes 16777216 | tf_op jit(solution)/shard_map/reshape | solution.py:90
  50.1 5.0 %copy.26 = f32[8,4,256,256]{2,0,3,1:T(8,128)S(1)} copy(f32[8,4,256,256]{2,1,0,3:T(4,128)} %reshape.117) | data formatting | bytes 16777216 | tf_op jit(solution)/shard_map/reshape | solution.py:90
  55.1 95.4 %all_to_all.5 = f32[8,4,256,256]{2,0,3,1:T(8,128)} all-to-all(f32[8,4,256,256]{2,0,3,1:T(8,128)S(1)} %copy.26), channel_id=1, replica_groups=mesh['dp'=8,'ctx'=4] {'ctx'}, dimensions={1} | all-to-all | bytes 16777216 | tf_op jit(solution)/shard_map/all_to_all | solution.py:91
  150.6 5.6 %reduce_sum.29 = f32[8,256,256]{1,0,2:T(8,128)} reduce(f32[8,4,256,256]{2,0,3,1:T(8,128)} %all_to_all.5, f32[]{:T(128)} %constant.11.clone.1), dimensions={1}, to_apply=%region_3.4 | reduce | flops 1572864 | bytes 10485764 | tf_op jit(solution)/shard_map/reduce_sum | solution.py:92
  156.2 2.9 %copy.35 = f32[8,256,256]{2,1,0:T(8,128)} copy(f32[8,256,256]{1,0,2:T(8,128)} %reduce_sum.29) | data formatting | bytes 4194304 | tf_op jit(solution)/shard_map/reshape | solution.py:92
  159.1 0.0 reduce-scatter.2.cloned.1.call-update
  159.1 0.3 fusion.6
  159.5 0.9 copy.29
  160.3 34.6 %reduce-scatter.2.cloned.1.call-done = f32[256,256]{1,0:T(8,128)} async-done(((f32[2048,256]{1,0:T(8,128)}), f32[256,256]{1,0:T(8,128)}) %reduce-scatter.2.cloned.1.call-update) | async-done | bytes 262160 | tf_op jit(solution)/shard_map/reduce_scatter | solution.py:93
  194.9 1.6 multiply_convert_fusion
  (4 shorter events, 0.0 us)
Async XLA Ops:
  7.2 27.7 %copy-start = (bf16[1,128,8192]{2,1,0:T(8,128)(2,1)S(1)}, bf16[1,128,8192]{2,1,0:T(8,128)(2,1)}, u32[]{:S(2)}) copy-start(bf16[1,128,8192]{2,1,0:T(8,128)(2,1)} %param.7) | copy-start | bytes 6291460
  7.2 187.7 %reduce-scatter.2.cloned.1.call-start = ((), (), s32[]{:S(2)}) async-start(), calls=%async_computation.2 | async-start | bytes 2359296 | tf_op jit(solution)/shard_map/reduce_scatter | solution.py:93
  8.1 12.9 %collective-permute-start.1 = (bf16[128,256]{1,0:T(8,128)(2,1)S(1)}, bf16[128,256]{1,0:T(8,128)(2,1)S(1)}, u32[]{:S(2)}, u32[]{:S(2)}) collective-permute-start(bf16[128,256]{1,0:T(8,128)(2,1)S(1)} %pad_maximum_fusion.1), channel_id=1, source_target_pairs={{0,1},{1,2},{2,3},{4,5},{5,6},{6,7},{8,9},{9,10},{10,11},{12,13},{... | collective-permute-start | bytes 196616 | tf_op jit(solution)/shard_map/ppermute | solution.py:12
  13.0 8.0 %collective-permute-start = (bf16[128,256]{1,0:T(8,128)(2,1)S(1)}, bf16[128,256]{1,0:T(8,128)(2,1)S(1)}, u32[]{:S(2)}, u32[]{:S(2)}) collective-permute-start(bf16[128,256]{1,0:T(8,128)(2,1)S(1)} %pad_maximum_fusion.1), channel_id=1, source_target_pairs={{0,2},{1,3},{4,6},{5,7},{8,10},{9,11},{12,14},{13,15},{16,18},{17,... | collective-permute-start | bytes 196616 | tf_op jit(solution)/shard_map/ppermute | solution.py:12
  23.7 1.9 copy-start.1
  26.7 6.9 %collective-permute-start.2 = (f32[128,256]{0,1:T(8,128)S(1)}, f32[128,256]{0,1:T(8,128)S(1)}, u32[]{:S(2)}, u32[]{:S(2)}) collective-permute-start(f32[128,256]{0,1:T(8,128)S(1)} %get-tuple-element.6), channel_id=1, source_target_pairs={{1,0},{2,1},{3,2},{5,4},{6,5},{7,6},{9,8},{10,9},{11,10},{13,12},{... | collective-permute-start | bytes 393224 | tf_op jit(solution)/shard_map/ppermute | solution.py:12
  28.0 6.9 %collective-permute-start.3 = (f32[128,256]{0,1:T(8,128)S(1)}, f32[128,256]{0,1:T(8,128)S(1)}, u32[]{:S(2)}, u32[]{:S(2)}) collective-permute-start(f32[128,256]{0,1:T(8,128)S(1)} %get-tuple-element.7), channel_id=1, source_target_pairs={{2,0},{3,1},{6,4},{7,5},{10,8},{11,9},{14,12},{15,13},{18,16},{19,... | collective-permute-start | bytes 393224 | tf_op jit(solution)/shard_map/ppermute | solution.py:12
Sparse Core Ops, SparseCore 0:
  159.2 35.5 reduce-scatter.1
where the time goes:
time: 204 us; the launch traced here: 203 us
  blocking collectives  95.4 us (47%)
  waiting for transfers between devices  40.2 us (20%)
  local copies, waits for them, and re-layouts  22.5 us (11%)
  between operations  14.8 us (7%)
  starting transfers between devices  10.9 us (5%)
  other arithmetic  10.2 us (5%)
  matrix products  9.29 us (5%)
    all_to_all x1, blocking collectives, shards(): lax.all_to_all(pieces, 'ctx', split_axis=1, concat_axis=1, tiled=True)  95.4 us
    reduce_scatter x1, waiting for transfers between devices, shards(): lax.psum_scatter(rollout_part, 'dp', scatter_dimension=0, tiled=True)  34.6 us
    reshape x2, local copies, waits for them, and re-layouts, shards(): partial_value.reshape(dp_count, ctx_count, slab_rows, 2 * head_size)  15.8 us
    ppermute x4, starting transfers between devices, passed_along(): return lax.ppermute(x, axis, pairs)  10.9 us
    reduce_sum x1, other arithmetic, shards(): jnp.sum(moved, axis=1).reshape(dp_count * slab_rows, 2 * head_size)  5.6 us
    ppermute x4, waiting for transfers between devices, passed_along(): return lax.ppermute(x, axis, pairs)  5.57 us
    dot_general x1, matrix products, shards(): jnp.einsum('rd,rc->dc', inputs_flat, grad_kv, preferred_element_type=jnp....  4.48 us
  transfers between devices with their start and end apart: 5, of which 3 were waited for; matrix products, arithmetic and copies ran while one was open for 2% of the time, Pallas kernels for 0%

commit v1 on v0

--- a/solution.py
+++ b/solution.py
@@ -1,9 +1,17 @@
+import functools
 import math
 
 import jax
 import jax.numpy as jnp
 from jax import lax
+from jax.experimental import pallas as pl
+from jax.experimental.pallas import tpu as pltpu
 from jax.sharding import PartitionSpec as P
+
+F32 = jnp.float32
+BF16 = jnp.bfloat16
+LOG2E = 1.4426950408889634
+NT = (((1,), (1,)), ((), ()))
 
 
 def passed_along(x, axis, by):
@@ -95,9 +103,299 @@
     return (grad_q.reshape(1, row_count, group_size * head_size), grad_weights)
 
 
+def fused_kernel(
+    n_dp, n_ctx, reach,
+    x_ref, q_ref, k_ref, v_ref, go_ref, seg_ref, len_ref,
+    gq_ref, gw_ref,
+    kbuf, vbuf, qs, gos, bias, p_low, ds_low, gsend, grecv, gkv_t, xbuf, csend, crecv, zsend, zrecv,
+    load_sem, xl_sem, kv_ss, kv_rs, g_ss, g_rs, a_ss, a_rs, x_ss, x_rs, c_ss, c_rs, z_ss, z_rs,
+):
+    rows = k_ref.shape[0]
+    head = k_ref.shape[1]
+    group = q_ref.shape[1] // head
+    slab = gw_ref.shape[0]
+    nz = n_dp // 2
+    window = reach * rows
+    scale = 1.0 / math.sqrt(head)
+    dp = lax.axis_index("dp")
+    ctx = lax.axis_index("ctx")
+    z = dp // 2
+    core = dp % 2
+    sibling = z * 2 + (1 - core)
+
+    def remote(src, dst, ss, rs, dp_to, ctx_to):
+        return pltpu.make_async_remote_copy(
+            src_ref=src, dst_ref=dst, send_sem=ss, recv_sem=rs,
+            device_id={"dp": dp_to, "ctx": ctx_to}, device_id_type=pl.DeviceIdType.MESH,
+        )
+
+    loads = []
+    for h in range(group):
+        cols = pl.ds(h * head, head)
+        loads.append(pltpu.make_async_copy(q_ref.at[:, cols], qs.at[pl.ds(h * rows, rows)], load_sem.at[2 * h]))
+        loads.append(pltpu.make_async_copy(go_ref.at[:, cols], gos.at[pl.ds(h * rows, rows)], load_sem.at[2 * h + 1]))
+    loads.append(pltpu.make_async_copy(k_ref, kbuf.at[pl.ds(window, rows)], load_sem.at[2 * group]))
+    loads.append(pltpu.make_async_copy(v_ref, vbuf.at[pl.ds(window, rows)], load_sem.at[2 * group + 1]))
+    for copy in loads:
+        copy.start()
+
+    barrier = pltpu.get_barrier_semaphore()
+    for o in range(1, n_ctx):
+        pl.semaphore_signal(barrier, inc=1, device_id={"dp": dp, "ctx": (ctx + o) % n_ctx}, device_id_type=pl.DeviceIdType.MESH)
+    pl.semaphore_signal(barrier, inc=1, device_id={"dp": sibling, "ctx": ctx}, device_id_type=pl.DeviceIdType.MESH)
+    for o in range(1, nz):
+        pl.semaphore_signal(barrier, inc=1, device_id={"dp": ((z + o) % nz) * 2 + core, "ctx": ctx}, device_id_type=pl.DeviceIdType.MESH)
+    pl.semaphore_wait(barrier, n_ctx - 1 + 1 + nz - 1)
+
+    def kv_copies(off, to):
+        slot = pl.ds((reach - off) * rows, rows)
+        return (
+            remote(k_ref, kbuf.at[slot], kv_ss.at[off - 1, 0], kv_rs.at[off - 1, 0], dp, to),
+            remote(v_ref, vbuf.at[slot], kv_ss.at[off - 1, 1], kv_rs.at[off - 1, 1], dp, to),
+        )
+
+    for off in range(1, reach + 1):
+        @pl.when(ctx + off < n_ctx)
+        def _():
+            for copy in kv_copies(off, (ctx + off) % n_ctx):
+                copy.start()
+
+    def piece_dp(k, s):
+        return ((z + 1 + k) % nz) * 2 + (1 - core if s == 0 else core)
+
+    def x_copy(k, s, o, source, to):
+        d = piece_dp(k, s)
+        cols = pl.ds(pl.multiple_of((d * n_ctx + to) * slab, slab), slab)
+        return remote(
+            x_ref.at[:, cols], xbuf.at[d, pl.ds(pl.multiple_of(source * rows, rows), rows)],
+            x_ss.at[k, s, o - 1], x_rs.at[k, s, o - 1], dp, to,
+        )
+
+    def x_local(k, s):
+        d = piece_dp(k, s)
+        cols = pl.ds(pl.multiple_of((d * n_ctx + ctx) * slab, slab), slab)
+        return pltpu.make_async_copy(
+            x_ref.at[:, cols], xbuf.at[d, pl.ds(pl.multiple_of(ctx * rows, rows), rows)], xl_sem.at[k, s]
+        )
+
+    for k in range(nz):
+        for s in range(2):
+            for o in range(1, n_ctx):
+                x_copy(k, s, o, ctx, (ctx + o) % n_ctx).start()
+            x_local(k, s).start()
+
+    length = len_ref[0]
+    key_at = lax.broadcasted_iota(jnp.int32, (rows, rows), 0)
+    query_at = lax.broadcasted_iota(jnp.int32, (rows, rows), 1) + ctx * rows
+    query_seg = seg_ref[:, pl.ds(pl.multiple_of(ctx * rows, rows), rows)].astype(F32)
+    for b in range(reach + 1):
+        first = (ctx - (reach - b)) * rows
+        from_row = pl.multiple_of(jnp.maximum(ctx - (reach - b), 0) * rows, rows)
+        key_seg = jnp.broadcast_to(seg_ref[:, pl.ds(from_row, rows)].astype(F32), (rows, rows)).T
+        key_pos = key_at + first
+        gap = query_at - key_pos
+        ok = (key_seg == query_seg) & (gap >= 0) & (gap < window) & (key_pos >= 0)
+        ok = ok & ((key_pos < length) | (gap == 0))
+        bias[pl.ds(b * rows, rows), :] = jnp.where(ok, 0.0, -1e30)
+    live = (lax.broadcasted_iota(jnp.int32, (1, rows), 1) + ctx * rows < length).astype(F32)
+
+    for off in range(1, reach + 1):
+        slot = pl.ds((reach - off) * rows, rows)
+
+        @pl.when(ctx - off < 0)
+        def _():
+            kbuf[slot, :] = jnp.zeros((rows, head), BF16)
+            vbuf[slot, :] = jnp.zeros((rows, head), BF16)
+
+    for copy in loads:
+        copy.wait()
+    for off in range(1, reach + 1):
+        @pl.when(ctx - off >= 0)
+        def _():
+            for copy in kv_copies(off, ctx):
+                copy.wait_recv()
+
+    for h in range(group):
+        here = pl.ds(h * rows, rows)
+        score = lax.dot_general(kbuf[...], qs[here, :], NT, preferred_element_type=F32) + bias[...]
+        top = jnp.max(score, axis=0, keepdims=True)
+        unnorm = jnp.exp2((score - top) * (scale * LOG2E))
+        probs = unnorm * (live / jnp.sum(unnorm, axis=0, keepdims=True))
+        p_low[:, here] = probs.astype(BF16)
+        dprobs = lax.dot_general(vbuf[...], gos[here, :], NT, preferred_element_type=F32)
+        row_dot = jnp.sum(probs * dprobs, axis=0, keepdims=True)
+        ds_low[:, here] = (probs * (dprobs - row_dot)).astype(BF16)
+
+    def kv_grad(b):
+        block = pl.ds(b * rows, rows)
+        gk = jnp.dot(ds_low[block, :], qs[...], preferred_element_type=F32) * scale
+        gv = jnp.dot(p_low[block, :], gos[...], preferred_element_type=F32)
+        return gk, gv
+
+    def g_copy(off, to):
+        return remote(gsend.at[off - 1], grecv.at[off - 1], g_ss.at[off - 1], g_rs.at[off - 1], dp, to)
+
+    for off in range(1, reach + 1):
+        gk, gv = kv_grad(reach - off)
+        gsend[off - 1, :, pl.ds(0, head)] = gk.astype(BF16)
+        gsend[off - 1, :, pl.ds(head, head)] = gv.astype(BF16)
+
+        @pl.when(ctx - off >= 0)
+        def _():
+            g_copy(off, (ctx + n_ctx - off) % n_ctx).start()
+
+        @pl.when(ctx + off >= n_ctx)
+        def _():
+            grecv[off - 1] = jnp.zeros((rows, 2 * head), BF16)
+
+    gk, gv = kv_grad(reach)
+
+    key_t = kbuf[...].astype(F32).T.astype(BF16)
+    for h in range(group):
+        here = pl.ds(h * rows, rows)
+        gq_t = jnp.dot(key_t, ds_low[:, here], preferred_element_type=F32) * scale
+        gq_ref[:, pl.ds(h * head, head)] = gq_t.T.astype(BF16)
+
+    for off in range(1, reach + 1):
+        @pl.when(ctx + off < n_ctx)
+        def _():
+            g_copy(off, ctx).wait_recv()
+    for off in range(1, reach + 1):
+        gk = gk + grecv[off - 1, :, pl.ds(0, head)].astype(F32)
+        gv = gv + grecv[off - 1, :, pl.ds(head, head)].astype(F32)
+    own = pl.ds(pl.multiple_of(ctx * rows, rows), rows)
+    gkv_t[pl.ds(0, head), own] = gk.T.astype(BF16)
+    gkv_t[pl.ds(head, head), own] = gv.T.astype(BF16)
+
+    def a_copy(o, source, to):
+        part = gkv_t.at[:, pl.ds(pl.multiple_of(source * rows, rows), rows)]
+        return remote(part, part, a_ss.at[o - 1], a_rs.at[o - 1], dp, to)
+
+    for o in range(1, n_ctx):
+        a_copy(o, ctx, (ctx + o) % n_ctx).start()
+    for o in range(1, n_ctx):
+        a_copy(o, (ctx + n_ctx - o) % n_ctx, ctx).wait_recv()
+
+    def product(k, s):
+        for o in range(1, n_ctx):
+            x_copy(k, s, o, (ctx + n_ctx - o) % n_ctx, ctx).wait_recv()
+        x_local(k, s).wait()
+        return jnp.dot(gkv_t[...], xbuf[piece_dp(k, s)], preferred_element_type=F32)
+
+    def c_copy(k):
+        return remote(csend.at[k], crecv.at[k], c_ss.at[k], c_rs.at[k], sibling, ctx)
+
+    def z_copy(k):
+        return remote(zsend.at[k], zrecv.at[k], z_ss.at[k], z_rs.at[k], piece_dp(k, 1), ctx)
+
+    total = None
+    for k in range(nz):
+        csend[k] = product(k, 0).astype(BF16)
+        c_copy(k).start()
+        part = product(k, 1)
+        c_copy(k).wait_recv()
+        part = part + crecv[k].astype(F32)
+        if k < nz - 1:
+            zsend[k] = part.astype(BF16)
+            z_copy(k).start()
+        else:
+            total = part
+    for k in range(nz - 1):
+        z_copy(k).wait_recv()
+        total = total + zrecv[k].astype(F32)
+    gw_ref[...] = (total * (1.0 / n_dp)).T.astype(BF16)
+
+    for off in range(1, reach + 1):
+        @pl.when(ctx + off < n_ctx)
+        def _():
+            for copy in kv_copies(off, (ctx + off) % n_ctx):
+                copy.wait_send()
+
+        @pl.when(ctx - off >= 0)
+        def _():
+            g_copy(off, (ctx + n_ctx - off) % n_ctx).wait_send()
+    for o in range(1, n_ctx):
+        a_copy(o, ctx, (ctx + o) % n_ctx).wait_send()
+    for k in range(nz):
+        for s in range(2):
+            for o in range(1, n_ctx):
+                x_copy(k, s, o, ctx, (ctx + o) % n_ctx).wait_send()
+        c_copy(k).wait_send()
+        if k < nz - 1:
+            z_copy(k).wait_send()
+
+
+def fused_shards(layer_input, queries, key_rows, value_rows, grad_output, segments, lengths):
+    n_dp = lax.axis_size("dp")
+    n_ctx = lax.axis_size("ctx")
+    rows, width = layer_input.shape[1:]
+    head = key_rows.shape[2]
+    group = queries.shape[2] // head
+    reach = min(8, n_ctx // 2)
+    keys = (reach + 1) * rows
+    slab = width // (n_dp * n_ctx)
+    nz = n_dp // 2
+    dma = pltpu.SemaphoreType.DMA
+    anywhere = pl.BlockSpec(memory_space=pl.ANY)
+    vmem = pl.BlockSpec(memory_space=pltpu.VMEM)
+    smem = pl.BlockSpec(memory_space=pltpu.SMEM)
+    gq, gw = pl.pallas_call(
+        functools.partial(fused_kernel, n_dp, n_ctx, reach),
+        out_shape=(
+            jax.ShapeDtypeStruct((rows, group * head), BF16),
+            jax.ShapeDtypeStruct((slab, 2 * head), BF16),
+        ),
+        in_specs=[anywhere] * 5 + [vmem, smem],
+        out_specs=(vmem, vmem),
+        scratch_shapes=[
+            pltpu.VMEM((keys, head), BF16),
+            pltpu.VMEM((keys, head), BF16),
+            pltpu.VMEM((group * rows, head), BF16),
+            pltpu.VMEM((group * rows, head), BF16),
+            pltpu.VMEM((keys, rows), F32),
+            pltpu.VMEM((keys, group * rows), BF16),
+            pltpu.VMEM((keys, group * rows), BF16),
+            pltpu.VMEM((reach, rows, 2 * head), BF16),
+            pltpu.VMEM((reach, rows, 2 * head), BF16),
+            pltpu.VMEM((2 * head, n_ctx * rows), BF16),
+            pltpu.VMEM((n_dp, n_ctx * rows, slab), BF16),
+            pltpu.VMEM((nz, 2 * head, slab), BF16),
+            pltpu.VMEM((nz, 2 * head, slab), BF16),
+            pltpu.VMEM((nz - 1, 2 * head, slab), BF16),
+            pltpu.VMEM((nz - 1, 2 * head, slab), BF16),
+            dma((2 * group + 2,)),
+            dma((nz, 2)),
+            dma((reach, 2)),
+            dma((reach, 2)),
+            dma((reach,)),
+            dma((reach,)),
+            dma((n_ctx - 1,)),
+            dma((n_ctx - 1,)),
+            dma((nz, 2, n_ctx - 1)),
+            dma((nz, 2, n_ctx - 1)),
+            dma((nz,)),
+            dma((nz,)),
+            dma((nz - 1,)),
+            dma((nz - 1,)),
+        ],
+        compiler_params=pltpu.CompilerParams(
+            collective_id=0, has_side_effects=True, vmem_limit_bytes=40 * 1024 * 1024
+        ),
+    )(layer_input[0], queries[0], key_rows[0], value_rows[0], grad_output[0], segments, lengths)
+    return gq[None], gw
+
+
+def by_size(layer_input, *rest):
+    n_dp, n_ctx = lax.axis_size("dp"), lax.axis_size("ctx")
+    slab = layer_input.shape[2] // (n_dp * n_ctx)
+    whole_tiles = slab % 128 == 0 and layer_input.shape[1] % 128 == 0
+    run = fused_shards if whole_tiles and n_dp % 2 == 0 and n_dp > 2 else shards
+    return run(layer_input, *rest)
+
+
 def solution(mesh):
     return jax.shard_map(
-        shards,
+        by_size,
         mesh=mesh,
         in_specs=(
             P("dp", "ctx", None),

time: 204 us -> 59.8 us (0.29)
  blocking collectives: 95.4 us -> 0 us
  Pallas kernels: 0 us -> 50.7 us
  waiting for transfers between devices: 40.2 us -> 0 us
  local copies, waits for them, and re-layouts: 22.5 us -> 7.04 us
  between operations: 14.8 us -> 1.3 us
  starting transfers between devices: 10.9 us -> 0 us
  other arithmetic: 10.2 us -> 0 us
  matrix products: 9.29 us -> 0 us
    all_to_all x1 -> x0, blocking collectives: 95.4 us -> none  [shards(): lax.all_to_all(pieces, 'ctx', split_axis=1, concat_axis=1, tiled=True)]
    pallas_call x0 -> x1, Pallas kernels: none -> 50.7 us  [fused_shards(): pl.pallas_call(functools.partial(fused_kernel, n_dp, n_ctx, reach), out_s...]
    reduce_scatter x1 -> x0, waiting for transfers between devices: 34.6 us -> none  [shards(): lax.psum_scatter(rollout_part, 'dp', scatter_dimension=0, tiled=True)]
    reshape x3 -> x0, local copies, waits for them, and re-layouts: 18.8 us -> none  [the longest x2 15.8 us: shards(): partial_value.reshape(dp_count, ctx_count, slab_rows, 2 * head_size)]
    ppermute x4 -> x0, starting transfers between devices: 10.9 us -> none  [passed_along(): return lax.ppermute(x, axis, pairs)]
    dot_general x5 -> x0, matrix products: 7.44 us -> none  [the longest x1 4.48 us: shards(): jnp.einsum('rd,rc->dc', inputs_flat, grad_kv, preferred_element_type=jnp....]
    unnamed x5 -> x14, local copies, waits for them, and re-layouts: 0.86 us -> 7.04 us
    reduce_sum x1 -> x0, other arithmetic: 5.6 us -> none  [shards(): jnp.sum(moved, axis=1).reshape(dp_count * slab_rows, 2 * head_size)]
  transfers between devices with their start and end apart: 5 -> 0, of which waited for: 3 -> 0; matrix products, arithmetic and copies ran while one was open for 2% -> 0% of each run, Pallas kernels for 0% -> 0%
where the time goes in v1:
time: 59.8 us; the launch traced here: 59 us
  Pallas kernels  50.7 us (85%)
  local copies, waits for them, and re-layouts  7.04 us (12%)
  between operations  1.3 us (2%)
    pallas_call x1, Pallas kernels, fused_shards(): pl.pallas_call(functools.partial(fused_kernel, n_dp, n_ctx, reach), out_s...  50.7 us
    unnamed x14, local copies, waits for them, and re-layouts  7.04 us

profile of v1, /device:TPU:0, one launch (start us, length us, event | category | flops | bytes accessed | tf_op | source)
XLA Modules:
  0.0 59.0 jit_solution(9849945375561405759)
XLA Ops:
  1.3 0.0 copy-start
  1.3 1.6 %copy-done = bf16[1,128,8192]{2,1,0:T(8,128)(2,1)S(1)} copy-done((bf16[1,128,8192]{2,1,0:T(8,128)(2,1)S(1)}, bf16[1,128,8192]{2,1,0:T(8,128)(2,1)}, u32[]{:S(2)}) %copy-start) | copy-done | bytes 2097176
  2.9 0.0 copy-start.1
  2.9 0.9 %copy-done.1 = bf16[1,128,1024]{2,1,0:T(8,128)(2,1)S(1)} copy-done((bf16[1,128,1024]{2,1,0:T(8,128)(2,1)S(1)}, bf16[1,128,1024]{2,1,0:T(8,128)(2,1)}, u32[]{:S(2)}) %copy-start.1) | copy-done | bytes 262168
  3.8 0.0 copy-start.2
  3.8 0.9 %copy-done.2 = bf16[1,128,1024]{2,1,0:T(8,128)(2,1)S(1)} copy-done((bf16[1,128,1024]{2,1,0:T(8,128)(2,1)S(1)}, bf16[1,128,1024]{2,1,0:T(8,128)(2,1)}, u32[]{:S(2)}) %copy-start.2) | copy-done | bytes 262168
  4.8 0.0 copy-start.3
  4.8 0.8 %copy-done.3 = bf16[1,128,128]{2,1,0:T(8,128)(2,1)S(1)} copy-done((bf16[1,128,128]{2,1,0:T(8,128)(2,1)S(1)}, bf16[1,128,128]{2,1,0:T(8,128)(2,1)}, u32[]{:S(2)}) %copy-start.3) | copy-done | bytes 32792
  5.5 0.0 copy-start.4
  5.5 0.8 %copy-done.4 = bf16[1,128,128]{2,1,0:T(8,128)(2,1)S(1)} copy-done((bf16[1,128,128]{2,1,0:T(8,128)(2,1)S(1)}, bf16[1,128,128]{2,1,0:T(8,128)(2,1)}, u32[]{:S(2)}) %copy-start.4) | copy-done | bytes 32792
  6.3 0.0 copy-start.5
  6.3 0.7 %copy-done.5 = s32[1,512]{1,0:T(1,128)S(1)} copy-done((s32[1,512]{1,0:T(1,128)S(1)}, s32[1,512]{1,0:T(1,128)}, u32[]{:S(2)}) %copy-start.5) | copy-done | bytes 2072
  7.0 50.7 %shard_map.86 = (bf16[128,1024]{1,0:T(8,128)(2,1)S(1)}, bf16[256,256]{1,0:T(8,128)(2,1)S(1)}) custom-call(bf16[128,8192]{1,0:T(8,128)(2,1)S(1)} %bitcast.6, bf16[128,1024]{1,0:T(8,128)(2,1)S(1)} %bitcast.7, bf16[128,128]{1,0:T(8,128)(2,1)S(1)} %bitcast.10, bf16[128,128]{1,0:T(8,128)(2,1)S(1)} %bitcast.11, bf16[128,1024]{1,0:T(8,128)(2,1)S(1)} %bitcast.8, ...), custom_call_target="tpu_custom_call" | custom-call | tf_op jit(solution)/shard_map/pallas_call | solution.py:342
  57.7 0.7 %copy.12 = bf16[1,128,1024]{2,1,0:T(8,128)(2,1)} copy(bf16[1,128,1024]{2,1,0:T(8,128)(2,1)S(1)} %bitcast.9) | data formatting | bytes 524288
  58.4 0.7 %copy.13 = bf16[256,256]{1,0:T(8,128)(2,1)} copy(bf16[256,256]{1,0:T(8,128)(2,1)S(1)} %get-tuple-element.9) | data formatting | bytes 262144
Async XLA Ops:
  1.3 1.6 %copy-start = (bf16[1,128,8192]{2,1,0:T(8,128)(2,1)S(1)}, bf16[1,128,8192]{2,1,0:T(8,128)(2,1)}, u32[]{:S(2)}) copy-start(bf16[1,128,8192]{2,1,0:T(8,128)(2,1)} %param.7) | copy-start | bytes 6291460
  2.9 0.9 %copy-start.1 = (bf16[1,128,1024]{2,1,0:T(8,128)(2,1)S(1)}, bf16[1,128,1024]{2,1,0:T(8,128)(2,1)}, u32[]{:S(2)}) copy-start(bf16[1,128,1024]{2,1,0:T(8,128)(2,1)} %param.8) | copy-start | bytes 786436
  3.8 0.9 %copy-start.2 = (bf16[1,128,1024]{2,1,0:T(8,128)(2,1)S(1)}, bf16[1,128,1024]{2,1,0:T(8,128)(2,1)}, u32[]{:S(2)}) copy-start(bf16[1,128,1024]{2,1,0:T(8,128)(2,1)} %param.11) | copy-start | bytes 786436
  4.8 0.8 %copy-start.3 = (bf16[1,128,128]{2,1,0:T(8,128)(2,1)S(1)}, bf16[1,128,128]{2,1,0:T(8,128)(2,1)}, u32[]{:S(2)}) copy-start(bf16[1,128,128]{2,1,0:T(8,128)(2,1)} %param.9) | copy-start | bytes 98308
  5.5 0.8 %copy-start.4 = (bf16[1,128,128]{2,1,0:T(8,128)(2,1)S(1)}, bf16[1,128,128]{2,1,0:T(8,128)(2,1)}, u32[]{:S(2)}) copy-start(bf16[1,128,128]{2,1,0:T(8,128)(2,1)} %param.10) | copy-start | bytes 98308
  6.3 0.7 %copy-start.5 = (s32[1,512]{1,0:T(1,128)S(1)}, s32[1,512]{1,0:T(1,128)}, u32[]{:S(2)}) copy-start(s32[1,512]{1,0:T(1,128)} %seg_ref.1) | copy-start | bytes 6148

commit v2 on v1

--- a/solution.py
+++ b/solution.py
@@ -178,11 +178,15 @@
             x_ref.at[:, cols], xbuf.at[d, pl.ds(pl.multiple_of(ctx * rows, rows), rows)], xl_sem.at[k, s]
         )
 
-    for k in range(nz):
-        for s in range(2):
+    pieces = [(k, s) for k in range(nz) for s in range(2)]
+
+    def issue(some):
+        for k, s in some:
             for o in range(1, n_ctx):
                 x_copy(k, s, o, ctx, (ctx + o) % n_ctx).start()
             x_local(k, s).start()
+
+    issue(pieces[:2])
 
     length = len_ref[0]
     key_at = lax.broadcasted_iota(jnp.int32, (rows, rows), 0)
@@ -216,6 +220,8 @@
                 copy.wait_recv()
 
     for h in range(group):
+        if h == group // 2:
+            issue(pieces[2:3])
         here = pl.ds(h * rows, rows)
         score = lax.dot_general(kbuf[...], qs[here, :], NT, preferred_element_type=F32) + bias[...]
         top = jnp.max(score, axis=0, keepdims=True)
@@ -248,6 +254,7 @@
         def _():
             grecv[off - 1] = jnp.zeros((rows, 2 * head), BF16)
 
+    issue(pieces[3:4])
     gk, gv = kv_grad(reach)
 
     key_t = kbuf[...].astype(F32).T.astype(BF16)
@@ -273,6 +280,7 @@
 
     for o in range(1, n_ctx):
         a_copy(o, ctx, (ctx + o) % n_ctx).start()
+    issue(pieces[4:])
     for o in range(1, n_ctx):
         a_copy(o, (ctx + n_ctx - o) % n_ctx, ctx).wait_recv()
 
@@ -288,10 +296,17 @@
     def z_copy(k):
         return remote(zsend.at[k], zrecv.at[k], z_ss.at[k], z_rs.at[k], piece_dp(k, 1), ctx)
 
-    total = None
-    for k in range(nz):
+    def to_sibling(k):
         csend[k] = product(k, 0).astype(BF16)
         c_copy(k).start()
+
+    total = None
+    to_sibling(0)
+    for k in range(nz):
+        if k == 0:
+            to_sibling(1)
+        elif k > 1:
+            to_sibling(k)
         part = product(k, 1)
         c_copy(k).wait_recv()
         part = part + crecv[k].astype(F32)
@@ -336,7 +351,7 @@
     slab = width // (n_dp * n_ctx)
     nz = n_dp // 2
     dma = pltpu.SemaphoreType.DMA
-    anywhere = pl.BlockSpec(memory_space=pl.ANY)
+    hbm = pl.BlockSpec(memory_space=pltpu.HBM)
     vmem = pl.BlockSpec(memory_space=pltpu.VMEM)
     smem = pl.BlockSpec(memory_space=pltpu.SMEM)
     gq, gw = pl.pallas_call(
@@ -345,7 +360,7 @@
             jax.ShapeDtypeStruct((rows, group * head), BF16),
             jax.ShapeDtypeStruct((slab, 2 * head), BF16),
         ),
-        in_specs=[anywhere] * 5 + [vmem, smem],
+        in_specs=[hbm] * 5 + [vmem, smem],
         out_specs=(vmem, vmem),
         scratch_shapes=[
             pltpu.VMEM((keys, head), BF16),

time: 59.8 us -> 48.7 us (0.81)
  Pallas kernels: 50.7 us -> 39.4 us
    pallas_call x1, Pallas kernels: 50.7 us -> 39.4 us  [fused_shards(): pl.pallas_call(functools.partial(fused_kernel, n_dp, n_ctx, reach), out_s...]
where the time goes in v2:
time: 48.7 us; the launch traced here: 47.7 us
  Pallas kernels  39.4 us (81%)
  local copies, waits for them, and re-layouts  7.04 us (14%)
  between operations  1.3 us (3%)
    pallas_call x1, Pallas kernels, fused_shards(): pl.pallas_call(functools.partial(fused_kernel, n_dp, n_ctx, reach), out_s...  39.4 us
    unnamed x14, local copies, waits for them, and re-layouts  7.04 us

profile of v2, /device:TPU:0, one launch (start us, length us, event | category | flops | bytes accessed | tf_op | source)
XLA Modules:
  0.0 47.7 jit_solution(11467124155325369368)
XLA Ops:
  1.3 0.0 copy-start
  1.3 1.6 %copy-done = bf16[1,128,8192]{2,1,0:T(8,128)(2,1)S(1)} copy-done((bf16[1,128,8192]{2,1,0:T(8,128)(2,1)S(1)}, bf16[1,128,8192]{2,1,0:T(8,128)(2,1)}, u32[]{:S(2)}) %copy-start) | copy-done | bytes 2097176
  2.9 0.0 copy-start.1
  2.9 0.9 %copy-done.1 = bf16[1,128,1024]{2,1,0:T(8,128)(2,1)S(1)} copy-done((bf16[1,128,1024]{2,1,0:T(8,128)(2,1)S(1)}, bf16[1,128,1024]{2,1,0:T(8,128)(2,1)}, u32[]{:S(2)}) %copy-start.1) | copy-done | bytes 262168
  3.8 0.0 copy-start.2
  3.8 0.9 %copy-done.2 = bf16[1,128,1024]{2,1,0:T(8,128)(2,1)S(1)} copy-done((bf16[1,128,1024]{2,1,0:T(8,128)(2,1)S(1)}, bf16[1,128,1024]{2,1,0:T(8,128)(2,1)}, u32[]{:S(2)}) %copy-start.2) | copy-done | bytes 262168
  4.8 0.0 copy-start.3
  4.8 0.8 %copy-done.3 = bf16[1,128,128]{2,1,0:T(8,128)(2,1)S(1)} copy-done((bf16[1,128,128]{2,1,0:T(8,128)(2,1)S(1)}, bf16[1,128,128]{2,1,0:T(8,128)(2,1)}, u32[]{:S(2)}) %copy-start.3) | copy-done | bytes 32792
  5.5 0.0 copy-start.4
  5.5 0.8 %copy-done.4 = bf16[1,128,128]{2,1,0:T(8,128)(2,1)S(1)} copy-done((bf16[1,128,128]{2,1,0:T(8,128)(2,1)S(1)}, bf16[1,128,128]{2,1,0:T(8,128)(2,1)}, u32[]{:S(2)}) %copy-start.4) | copy-done | bytes 32792
  6.3 0.0 copy-start.5
  6.3 0.7 %copy-done.5 = s32[1,512]{1,0:T(1,128)S(1)} copy-done((s32[1,512]{1,0:T(1,128)S(1)}, s32[1,512]{1,0:T(1,128)}, u32[]{:S(2)}) %copy-start.5) | copy-done | bytes 2072
  7.0 39.4 %shard_map.86 = (bf16[128,1024]{1,0:T(8,128)(2,1)S(1)}, bf16[256,256]{1,0:T(8,128)(2,1)S(1)}) custom-call(bf16[128,8192]{1,0:T(8,128)(2,1)S(1)} %bitcast.6, bf16[128,1024]{1,0:T(8,128)(2,1)S(1)} %bitcast.7, bf16[128,128]{1,0:T(8,128)(2,1)S(1)} %bitcast.10, bf16[128,128]{1,0:T(8,128)(2,1)S(1)} %bitcast.11, bf16[128,1024]{1,0:T(8,128)(2,1)S(1)} %bitcast.8, ...), custom_call_target="tpu_custom_call" | custom-call | tf_op jit(solution)/shard_map/pallas_call | solution.py:357
  46.3 0.7 %copy.12 = bf16[1,128,1024]{2,1,0:T(8,128)(2,1)} copy(bf16[1,128,1024]{2,1,0:T(8,128)(2,1)S(1)} %bitcast.9) | data formatting | bytes 524288
  47.0 0.7 %copy.13 = bf16[256,256]{1,0:T(8,128)(2,1)} copy(bf16[256,256]{1,0:T(8,128)(2,1)S(1)} %get-tuple-element.9) | data formatting | bytes 262144
Async XLA Ops:
  1.3 1.6 %copy-start = (bf16[1,128,8192]{2,1,0:T(8,128)(2,1)S(1)}, bf16[1,128,8192]{2,1,0:T(8,128)(2,1)}, u32[]{:S(2)}) copy-start(bf16[1,128,8192]{2,1,0:T(8,128)(2,1)} %param.7) | copy-start | bytes 6291460
  2.9 0.9 %copy-start.1 = (bf16[1,128,1024]{2,1,0:T(8,128)(2,1)S(1)}, bf16[1,128,1024]{2,1,0:T(8,128)(2,1)}, u32[]{:S(2)}) copy-start(bf16[1,128,1024]{2,1,0:T(8,128)(2,1)} %param.8) | copy-start | bytes 786436
  3.8 0.9 %copy-start.2 = (bf16[1,128,1024]{2,1,0:T(8,128)(2,1)S(1)}, bf16[1,128,1024]{2,1,0:T(8,128)(2,1)}, u32[]{:S(2)}) copy-start(bf16[1,128,1024]{2,1,0:T(8,128)(2,1)} %param.11) | copy-start | bytes 786436
  4.8 0.8 %copy-start.3 = (bf16[1,128,128]{2,1,0:T(8,128)(2,1)S(1)}, bf16[1,128,128]{2,1,0:T(8,128)(2,1)}, u32[]{:S(2)}) copy-start(bf16[1,128,128]{2,1,0:T(8,128)(2,1)} %param.9) | copy-start | bytes 98308
  5.5 0.8 %copy-start.4 = (bf16[1,128,128]{2,1,0:T(8,128)(2,1)S(1)}, bf16[1,128,128]{2,1,0:T(8,128)(2,1)}, u32[]{:S(2)}) copy-start(bf16[1,128,128]{2,1,0:T(8,128)(2,1)} %param.10) | copy-start | bytes 98308
  6.3 0.7 %copy-start.5 = (s32[1,512]{1,0:T(1,128)S(1)}, s32[1,512]{1,0:T(1,128)}, u32[]{:S(2)}) copy-start(s32[1,512]{1,0:T(1,128)} %seg_ref.1) | copy-start | bytes 6148

commit v3 on v2

--- a/solution.py
+++ b/solution.py
@@ -186,7 +186,7 @@
                 x_copy(k, s, o, ctx, (ctx + o) % n_ctx).start()
             x_local(k, s).start()
 
-    issue(pieces[:2])
+    issue(pieces[:3])
 
     length = len_ref[0]
     key_at = lax.broadcasted_iota(jnp.int32, (rows, rows), 0)
@@ -221,7 +221,7 @@
 
     for h in range(group):
         if h == group // 2:
-            issue(pieces[2:3])
+            issue(pieces[3:4])
         here = pl.ds(h * rows, rows)
         score = lax.dot_general(kbuf[...], qs[here, :], NT, preferred_element_type=F32) + bias[...]
         top = jnp.max(score, axis=0, keepdims=True)
@@ -254,7 +254,7 @@
         def _():
             grecv[off - 1] = jnp.zeros((rows, 2 * head), BF16)
 
-    issue(pieces[3:4])
+    issue(pieces[4:5])
     gk, gv = kv_grad(reach)
 
     key_t = kbuf[...].astype(F32).T.astype(BF16)
@@ -280,7 +280,7 @@
 
     for o in range(1, n_ctx):
         a_copy(o, ctx, (ctx + o) % n_ctx).start()
-    issue(pieces[4:])
+    issue(pieces[5:])
     for o in range(1, n_ctx):
         a_copy(o, (ctx + n_ctx - o) % n_ctx, ctx).wait_recv()
 
@@ -394,7 +394,7 @@
             dma((nz - 1,)),
         ],
         compiler_params=pltpu.CompilerParams(
-            collective_id=0, has_side_effects=True, vmem_limit_bytes=40 * 1024 * 1024
+            collective_id=0, has_side_effects=True, vmem_limit_bytes=62 * 1024 * 1024
         ),
     )(layer_input[0], queries[0], key_rows[0], value_rows[0], grad_output[0], segments, lengths)
     return gq[None], gw

time: 48.7 us -> 48.9 us (level)
  Pallas kernels: 39.4 us -> 43.6 us
  local copies, waits for them, and re-layouts: 7.04 us -> 3.24 us
    pallas_call x1, Pallas kernels: 39.4 us -> 43.6 us  [fused_shards(): pl.pallas_call(functools.partial(fused_kernel, n_dp, n_ctx, reach), out_s...]
    unnamed x14 -> x2, local copies, waits for them, and re-layouts: 7.04 us -> 3.24 us
where the time goes in v3:
time: 48.9 us; the launch traced here: 48.1 us
  Pallas kernels  43.6 us (89%)
  local copies, waits for them, and re-layouts  3.24 us (7%)
  between operations  1.29 us (3%)
    pallas_call x1, Pallas kernels, fused_shards(): pl.pallas_call(functools.partial(fused_kernel, n_dp, n_ctx, reach), out_s...  43.6 us
    unnamed x2, local copies, waits for them, and re-layouts  3.24 us

profile of v3, /device:TPU:0, one launch (start us, length us, event | category | flops | bytes accessed | tf_op | source)
XLA Modules:
  0.0 48.1 jit_solution(17752314200942309370)
XLA Ops:
  1.3 43.6 %shard_map.86 = (bf16[128,1024]{1,0:T(8,128)(2,1)}, bf16[256,256]{1,0:T(8,128)(2,1)}) custom-call(bf16[128,8192]{1,0:T(8,128)(2,1)} %bitcast.6, bf16[128,1024]{1,0:T(8,128)(2,1)} %bitcast.7, bf16[128,128]{1,0:T(8,128)(2,1)} %bitcast.10, bf16[128,128]{1,0:T(8,128)(2,1)} %bitcast.11, bf16[128,1024]{1,0:T(8,128)(2,1)} %bitcast.8, s32[1,512]{1,0:T(1,128)} %seg_ref.1, ...), custom_call_target="tpu_custom_call" | custom-call | tf_op jit(solution)/shard_map/pallas_call | solution.py:357
  44.9 1.7 %copy.12 = bf16[1,128,1024]{2,1,0:T(8,128)(2,1)} copy(bf16[1,128,1024]{2,1,0:T(8,128)(2,1)} %bitcast.9) | data formatting | bytes 524288
  46.5 1.6 %copy.13 = bf16[256,256]{1,0:T(8,128)(2,1)} copy(bf16[256,256]{1,0:T(8,128)(2,1)} %get-tuple-element.9) | data formatting | bytes 262144

commit v4 on v3

--- a/solution.py
+++ b/solution.py
@@ -186,7 +186,7 @@
                 x_copy(k, s, o, ctx, (ctx + o) % n_ctx).start()
             x_local(k, s).start()
 
-    issue(pieces[:3])
+    issue(pieces[:1])
 
     length = len_ref[0]
     key_at = lax.broadcasted_iota(jnp.int32, (rows, rows), 0)
@@ -221,7 +221,7 @@
 
     for h in range(group):
         if h == group // 2:
-            issue(pieces[3:4])
+            issue(pieces[1:2])
         here = pl.ds(h * rows, rows)
         score = lax.dot_general(kbuf[...], qs[here, :], NT, preferred_element_type=F32) + bias[...]
         top = jnp.max(score, axis=0, keepdims=True)
@@ -254,7 +254,7 @@
         def _():
             grecv[off - 1] = jnp.zeros((rows, 2 * head), BF16)
 
-    issue(pieces[4:5])
+    issue(pieces[2:3])
     gk, gv = kv_grad(reach)
 
     key_t = kbuf[...].astype(F32).T.astype(BF16)
@@ -280,7 +280,7 @@
 
     for o in range(1, n_ctx):
         a_copy(o, ctx, (ctx + o) % n_ctx).start()
-    issue(pieces[5:])
+    issue(pieces[3:])
     for o in range(1, n_ctx):
         a_copy(o, (ctx + n_ctx - o) % n_ctx, ctx).wait_recv()
 
@@ -338,6 +338,17 @@
         c_copy(k).wait_send()
         if k < nz - 1:
             z_copy(k).wait_send()
+
+
+def hand_over(gq_from, gw_from, gq_to, gw_to, sem):
+    copies = [
+        pltpu.make_async_copy(gq_from, gq_to, sem.at[0]),
+        pltpu.make_async_copy(gw_from, gw_to, sem.at[1]),
+    ]
+    for copy in copies:
+        copy.start()
+    for copy in copies:
+        copy.wait()
 
 
 def fused_shards(layer_input, queries, key_rows, value_rows, grad_output, segments, lengths):
@@ -397,6 +408,14 @@
             collective_id=0, has_side_effects=True, vmem_limit_bytes=62 * 1024 * 1024
         ),
     )(layer_input[0], queries[0], key_rows[0], value_rows[0], grad_output[0], segments, lengths)
+    gq, gw = pl.pallas_call(
+        hand_over,
+        out_shape=(jax.ShapeDtypeStruct(gq.shape, BF16), jax.ShapeDtypeStruct(gw.shape, BF16)),
+        in_specs=[hbm] * 2,
+        out_specs=(hbm, hbm),
+        scratch_shapes=[dma((2,))],
+        compiler_params=pltpu.CompilerParams(vmem_limit_bytes=62 * 1024 * 1024),
+    )(gq, gw)
     return gq[None], gw
 
 

time: 48.9 us -> 57.4 us (1.17)
  Pallas kernels: 43.6 us -> 55.9 us
  local copies, waits for them, and re-layouts: 3.24 us -> 0 us
    pallas_call x0 -> x1, Pallas kernels: none -> 13 us  [fused_shards(): pl.pallas_call(hand_over, out_shape=(jax.ShapeDtypeStruct(gq.shape, BF16)...]
    unnamed x2 -> x0, local copies, waits for them, and re-layouts: 3.24 us -> none
    pallas_call x1, Pallas kernels: 43.6 us -> 42.8 us  [fused_shards(): pl.pallas_call(functools.partial(fused_kernel, n_dp, n_ctx, reach), out_s...]
where the time goes in v4:
time: 57.4 us; the launch traced here: 57.2 us
  Pallas kernels  55.9 us (97%)
  between operations  1.29 us (2%)
    pallas_call x1, Pallas kernels, fused_shards(): pl.pallas_call(functools.partial(fused_kernel, n_dp, n_ctx, reach), out_s...  42.8 us
    pallas_call x1, Pallas kernels, fused_shards(): pl.pallas_call(hand_over, out_shape=(jax.ShapeDtypeStruct(gq.shape, BF16)...  13 us

profile of v4, /device:TPU:0, one launch (start us, length us, event | category | flops | bytes accessed | tf_op | source)
XLA Modules:
  0.0 57.2 jit_solution(10710439220588653908)
XLA Ops:
  1.3 42.8 %shard_map.86 = (bf16[128,1024]{1,0:T(8,128)(2,1)}, bf16[256,256]{1,0:T(8,128)(2,1)}) custom-call(bf16[128,8192]{1,0:T(8,128)(2,1)} %bitcast.6, bf16[128,1024]{1,0:T(8,128)(2,1)} %bitcast.7, bf16[128,128]{1,0:T(8,128)(2,1)} %bitcast.9, bf16[128,128]{1,0:T(8,128)(2,1)} %bitcast.10, bf16[128,1024]{1,0:T(8,128)(2,1)} %bitcast.8, s32[1,512]{1,0:T(1,128)} %seg_ref.1, ...), custom_call_target="tpu_custom_call" | custom-call | tf_op jit(solution)/shard_map/pallas_call | solution.py:368
  44.1 13.0 %shard_map.87 = (bf16[128,1024]{1,0:T(8,128)(2,1)}, bf16[256,256]{1,0:T(8,128)(2,1)}) custom-call(bf16[128,1024]{1,0:T(8,128)(2,1)} %get-tuple-element.6.gq_from, bf16[256,256]{1,0:T(8,128)(2,1)} %get-tuple-element.7.gw_from), custom_call_target="tpu_custom_call" | custom-call | tf_op jit(solution)/shard_map/pallas_call | solution.py:411

commit v5 on v2

--- a/solution.py
+++ b/solution.py
@@ -107,8 +107,8 @@
     n_dp, n_ctx, reach,
     x_ref, q_ref, k_ref, v_ref, go_ref, seg_ref, len_ref,
     gq_ref, gw_ref,
-    kbuf, vbuf, qs, gos, bias, p_low, ds_low, gsend, grecv, gkv_t, xbuf, csend, crecv, zsend, zrecv,
-    load_sem, xl_sem, kv_ss, kv_rs, g_ss, g_rs, a_ss, a_rs, x_ss, x_rs, c_ss, c_rs, z_ss, z_rs,
+    xin, kbuf, vbuf, qs, gos, bias, p_low, ds_low, gsend, grecv, gkv_t, xbuf, csend, crecv, zsend, zrecv,
+    xin_sem, load_sem, xl_sem, kv_ss, kv_rs, g_ss, g_rs, a_ss, a_rs, x_ss, x_rs, c_ss, c_rs, z_ss, z_rs,
 ):
     rows = k_ref.shape[0]
     head = k_ref.shape[1]
@@ -139,6 +139,14 @@
     for copy in loads:
         copy.start()
 
+    def x_load(k):
+        wide = 2 * n_ctx * slab
+        cols = pl.ds(pl.multiple_of(((z + 1 + k) % nz) * wide, wide), wide)
+        return pltpu.make_async_copy(x_ref.at[:, cols], xin.at[:, cols], xin_sem.at[k])
+
+    for k in range(nz):
+        x_load(k).start()
+
     barrier = pltpu.get_barrier_semaphore()
     for o in range(1, n_ctx):
         pl.semaphore_signal(barrier, inc=1, device_id={"dp": dp, "ctx": (ctx + o) % n_ctx}, device_id_type=pl.DeviceIdType.MESH)
@@ -167,7 +175,7 @@
         d = piece_dp(k, s)
         cols = pl.ds(pl.multiple_of((d * n_ctx + to) * slab, slab), slab)
         return remote(
-            x_ref.at[:, cols], xbuf.at[d, pl.ds(pl.multiple_of(source * rows, rows), rows)],
+            xin.at[:, cols], xbuf.at[d, pl.ds(pl.multiple_of(source * rows, rows), rows)],
             x_ss.at[k, s, o - 1], x_rs.at[k, s, o - 1], dp, to,
         )
 
@@ -175,13 +183,15 @@
         d = piece_dp(k, s)
         cols = pl.ds(pl.multiple_of((d * n_ctx + ctx) * slab, slab), slab)
         return pltpu.make_async_copy(
-            x_ref.at[:, cols], xbuf.at[d, pl.ds(pl.multiple_of(ctx * rows, rows), rows)], xl_sem.at[k, s]
+            xin.at[:, cols], xbuf.at[d, pl.ds(pl.multiple_of(ctx * rows, rows), rows)], xl_sem.at[k, s]
         )
 
     pieces = [(k, s) for k in range(nz) for s in range(2)]
 
     def issue(some):
         for k, s in some:
+            if s == 0:
+                x_load(k).wait()
             for o in range(1, n_ctx):
                 x_copy(k, s, o, ctx, (ctx + o) % n_ctx).start()
             x_local(k, s).start()
@@ -338,6 +348,11 @@
         c_copy(k).wait_send()
         if k < nz - 1:
             z_copy(k).wait_send()
+
+
+def hand_over(gq_from, gw_from, gq_to, gw_to):
+    gq_to[...] = gq_from[...]
+    gw_to[...] = gw_from[...]
 
 
 def fused_shards(layer_input, queries, key_rows, value_rows, grad_output, segments, lengths):
@@ -363,6 +378,7 @@
         in_specs=[hbm] * 5 + [vmem, smem],
         out_specs=(vmem, vmem),
         scratch_shapes=[
+            pltpu.VMEM((rows, width), BF16),
             pltpu.VMEM((keys, head), BF16),
             pltpu.VMEM((keys, head), BF16),
             pltpu.VMEM((group * rows, head), BF16),
@@ -378,6 +394,7 @@
             pltpu.VMEM((nz, 2 * head, slab), BF16),
             pltpu.VMEM((nz - 1, 2 * head, slab), BF16),
             pltpu.VMEM((nz - 1, 2 * head, slab), BF16),
+            dma((nz,)),
             dma((2 * group + 2,)),
             dma((nz, 2)),
             dma((reach, 2)),
@@ -394,9 +411,16 @@
             dma((nz - 1,)),
         ],
         compiler_params=pltpu.CompilerParams(
-            collective_id=0, has_side_effects=True, vmem_limit_bytes=40 * 1024 * 1024
+            collective_id=0, has_side_effects=True, vmem_limit_bytes=62 * 1024 * 1024
         ),
     )(layer_input[0], queries[0], key_rows[0], value_rows[0], grad_output[0], segments, lengths)
+    gq, gw = pl.pallas_call(
+        hand_over,
+        out_shape=(jax.ShapeDtypeStruct(gq.shape, BF16), jax.ShapeDtypeStruct(gw.shape, BF16)),
+        in_specs=[vmem] * 2,
+        out_specs=(vmem, vmem),
+        compiler_params=pltpu.CompilerParams(vmem_limit_bytes=62 * 1024 * 1024),
+    )(gq, gw)
     return gq[None], gw
 
 

time: 48.7 us -> 44.5 us (0.914)
  local copies, waits for them, and re-layouts: 7.04 us -> 0 us
  Pallas kernels: 39.4 us -> 42.5 us
    unnamed x14 -> x0, local copies, waits for them, and re-layouts: 7.04 us -> none
    pallas_call x0 -> x1, Pallas kernels: none -> 1.74 us  [fused_shards(): pl.pallas_call(hand_over, out_shape=(jax.ShapeDtypeStruct(gq.shape, BF16)...]
    pallas_call x1, Pallas kernels: 39.4 us -> 40.7 us  [fused_shards(): pl.pallas_call(functools.partial(fused_kernel, n_dp, n_ctx, reach), out_s...]
where the time goes in v5:
time: 44.5 us; the launch traced here: 43.8 us
  Pallas kernels  42.5 us (96%)
  between operations  1.29 us (3%)
    pallas_call x1, Pallas kernels, fused_shards(): pl.pallas_call(functools.partial(fused_kernel, n_dp, n_ctx, reach), out_s...  40.7 us
    pallas_call x1, Pallas kernels, fused_shards(): pl.pallas_call(hand_over, out_shape=(jax.ShapeDtypeStruct(gq.shape, BF16)...  1.74 us

profile of v5, /device:TPU:0, one launch (start us, length us, event | category | flops | bytes accessed | tf_op | source)
XLA Modules:
  0.0 43.8 jit_solution(10424780314492242427)
XLA Ops:
  1.3 40.7 %shard_map.86 = (bf16[128,1024]{1,0:T(8,128)(2,1)}, bf16[256,256]{1,0:T(8,128)(2,1)}) custom-call(bf16[128,8192]{1,0:T(8,128)(2,1)} %bitcast.6, bf16[128,1024]{1,0:T(8,128)(2,1)} %bitcast.7, bf16[128,128]{1,0:T(8,128)(2,1)} %bitcast.9, bf16[128,128]{1,0:T(8,128)(2,1)} %bitcast.10, bf16[128,1024]{1,0:T(8,128)(2,1)} %bitcast.8, s32[1,512]{1,0:T(1,128)} %seg_ref.1, ...), custom_call_target="tpu_custom_call" | custom-call | tf_op jit(solution)/shard_map/pallas_call | solution.py:372
  42.0 1.7 %shard_map.87 = (bf16[128,1024]{1,0:T(8,128)(2,1)}, bf16[256,256]{1,0:T(8,128)(2,1)}) custom-call(bf16[128,1024]{1,0:T(8,128)(2,1)} %get-tuple-element.6.gq_from, bf16[256,256]{1,0:T(8,128)(2,1)} %get-tuple-element.7.gw_from), custom_call_target="tpu_custom_call" | custom-call | tf_op jit(solution)/shard_map/pallas_call | solution.py:417

commit v6 on v5

--- a/solution.py
+++ b/solution.py
@@ -122,6 +122,15 @@
     z = dp // 2
     core = dp % 2
     sibling = z * 2 + (1 - core)
+    ny = n_ctx // 2
+    row, col = ctx // 2, ctx % 2
+
+    def peer_to(m):
+        return ((row + m // 2) % ny) * 2 + (col + m % 2) % 2
+
+    def peer_from(m):
+        return ((row + ny - m // 2) % ny) * 2 + (col + m % 2) % 2
+
 
     def remote(src, dst, ss, rs, dp_to, ctx_to):
         return pltpu.make_async_remote_copy(
@@ -192,8 +201,9 @@
         for k, s in some:
             if s == 0:
                 x_load(k).wait()
-            for o in range(1, n_ctx):
-                x_copy(k, s, o, ctx, (ctx + o) % n_ctx).start()
+            for j in range(n_ctx - 1):
+                m = 1 + (j + core) % 2 if j < 2 else j + 1
+                x_copy(k, s, m, ctx, peer_to(m)).start()
             x_local(k, s).start()
 
     issue(pieces[:2])
@@ -289,14 +299,14 @@
         return remote(part, part, a_ss.at[o - 1], a_rs.at[o - 1], dp, to)
 
     for o in range(1, n_ctx):
-        a_copy(o, ctx, (ctx + o) % n_ctx).start()
+        a_copy(o, ctx, peer_to(o)).start()
     issue(pieces[4:])
     for o in range(1, n_ctx):
-        a_copy(o, (ctx + n_ctx - o) % n_ctx, ctx).wait_recv()
+        a_copy(o, peer_from(o), ctx).wait_recv()
 
     def product(k, s):
         for o in range(1, n_ctx):
-            x_copy(k, s, o, (ctx + n_ctx - o) % n_ctx, ctx).wait_recv()
+            x_copy(k, s, o, peer_from(o), ctx).wait_recv()
         x_local(k, s).wait()
         return jnp.dot(gkv_t[...], xbuf[piece_dp(k, s)], preferred_element_type=F32)
 
@@ -340,11 +350,11 @@
         def _():
             g_copy(off, (ctx + n_ctx - off) % n_ctx).wait_send()
     for o in range(1, n_ctx):
-        a_copy(o, ctx, (ctx + o) % n_ctx).wait_send()
+        a_copy(o, ctx, peer_to(o)).wait_send()
     for k in range(nz):
         for s in range(2):
             for o in range(1, n_ctx):
-                x_copy(k, s, o, ctx, (ctx + o) % n_ctx).wait_send()
+                x_copy(k, s, o, ctx, peer_to(o)).wait_send()
         c_copy(k).wait_send()
         if k < nz - 1:
             z_copy(k).wait_send()
@@ -428,7 +438,7 @@
     n_dp, n_ctx = lax.axis_size("dp"), lax.axis_size("ctx")
     slab = layer_input.shape[2] // (n_dp * n_ctx)
     whole_tiles = slab % 128 == 0 and layer_input.shape[1] % 128 == 0
-    run = fused_shards if whole_tiles and n_dp % 2 == 0 and n_dp > 2 else shards
+    run = fused_shards if whole_tiles and n_dp % 2 == 0 and n_ctx % 2 == 0 and min(n_dp, n_ctx) > 2 else shards
     return run(layer_input, *rest)
 
 

time: 44.5 us -> 44.1 us (level)
  the two profiles are of different devices: /device:TPU:0 before, /device:TPU:29 now
where the time goes in v6:
time: 44.1 us; the launch traced here: 43.9 us
  Pallas kernels  42.6 us (97%)
  between operations  1.29 us (3%)
    pallas_call x1, Pallas kernels, fused_shards(): pl.pallas_call(functools.partial(fused_kernel, n_dp, n_ctx, reach), out_s...  40.8 us
    pallas_call x1, Pallas kernels, fused_shards(): pl.pallas_call(hand_over, out_shape=(jax.ShapeDtypeStruct(gq.shape, BF16)...  1.74 us

profile of v6, /device:TPU:29, one launch (start us, length us, event | category | flops | bytes accessed | tf_op | source)
XLA Modules:
  0.0 43.9 jit_solution(8686623843137541895)
XLA Ops:
  1.3 40.8 %shard_map.86 = (bf16[128,1024]{1,0:T(8,128)(2,1)}, bf16[256,256]{1,0:T(8,128)(2,1)}) custom-call(bf16[128,8192]{1,0:T(8,128)(2,1)} %bitcast.6, bf16[128,1024]{1,0:T(8,128)(2,1)} %bitcast.7, bf16[128,128]{1,0:T(8,128)(2,1)} %bitcast.9, bf16[128,128]{1,0:T(8,128)(2,1)} %bitcast.10, bf16[128,1024]{1,0:T(8,128)(2,1)} %bitcast.8, s32[1,512]{1,0:T(1,128)} %seg_ref.1, ...), custom_call_target="tpu_custom_call" | custom-call | tf_op jit(solution)/shard_map/pallas_call | solution.py:382
  42.1 1.7 %shard_map.87 = (bf16[128,1024]{1,0:T(8,128)(2,1)}, bf16[256,256]{1,0:T(8,128)(2,1)}) custom-call(bf16[128,1024]{1,0:T(8,128)(2,1)} %get-tuple-element.6.gq_from, bf16[256,256]{1,0:T(8,128)(2,1)} %get-tuple-element.7.gw_from), custom_call_target="tpu_custom_call" | custom-call | tf_op jit(solution)/shard_map/pallas_call | solution.py:427

commit v7 on v6

--- a/solution.py
+++ b/solution.py
@@ -148,20 +148,37 @@
     for copy in loads:
         copy.start()
 
-    def x_load(k):
-        wide = 2 * n_ctx * slab
-        cols = pl.ds(pl.multiple_of(((z + 1 + k) % nz) * wide, wide), wide)
-        return pltpu.make_async_copy(x_ref.at[:, cols], xin.at[:, cols], xin_sem.at[k])
-
-    for k in range(nz):
-        x_load(k).start()
-
     barrier = pltpu.get_barrier_semaphore()
     for o in range(1, n_ctx):
         pl.semaphore_signal(barrier, inc=1, device_id={"dp": dp, "ctx": (ctx + o) % n_ctx}, device_id_type=pl.DeviceIdType.MESH)
     pl.semaphore_signal(barrier, inc=1, device_id={"dp": sibling, "ctx": ctx}, device_id_type=pl.DeviceIdType.MESH)
     for o in range(1, nz):
         pl.semaphore_signal(barrier, inc=1, device_id={"dp": ((z + o) % nz) * 2 + core, "ctx": ctx}, device_id_type=pl.DeviceIdType.MESH)
+
+    def piece_dp(k, s):
+        return ((z + 1 + k) % nz) * 2 + (1 - core if s == 0 else core)
+
+    def x_cols(d, to):
+        return pl.ds(pl.multiple_of((d * n_ctx + to) * slab, slab), slab)
+
+    def x_pack(k, s, m):
+        d = piece_dp(k, s)
+        return pltpu.make_async_copy(x_ref.at[:, x_cols(d, peer_to(m))], xin.at[d, peer_to(m)], xin_sem.at[k, s, m - 1])
+
+    def x_local(k, s):
+        d = piece_dp(k, s)
+        mine = pl.ds(pl.multiple_of(ctx * rows, rows), rows)
+        return pltpu.make_async_copy(x_ref.at[:, x_cols(d, ctx)], xbuf.at[d, mine], xl_sem.at[k, s])
+
+    pieces = [(k, s) for k in range(nz) for s in range(2)]
+
+    def pack(some):
+        for k, s in some:
+            for m in range(1, n_ctx):
+                x_pack(k, s, m).start()
+            x_local(k, s).start()
+
+    pack(pieces[:2])
     pl.semaphore_wait(barrier, n_ctx - 1 + 1 + nz - 1)
 
     def kv_copies(off, to):
@@ -177,36 +194,23 @@
             for copy in kv_copies(off, (ctx + off) % n_ctx):
                 copy.start()
 
-    def piece_dp(k, s):
-        return ((z + 1 + k) % nz) * 2 + (1 - core if s == 0 else core)
-
-    def x_copy(k, s, o, source, to):
+    def x_copy(k, s, m, source, to):
         d = piece_dp(k, s)
-        cols = pl.ds(pl.multiple_of((d * n_ctx + to) * slab, slab), slab)
         return remote(
-            xin.at[:, cols], xbuf.at[d, pl.ds(pl.multiple_of(source * rows, rows), rows)],
-            x_ss.at[k, s, o - 1], x_rs.at[k, s, o - 1], dp, to,
+            xin.at[d, to], xbuf.at[d, pl.ds(pl.multiple_of(source * rows, rows), rows)],
+            x_ss.at[k, s, m - 1], x_rs.at[k, s, m - 1], dp, to,
         )
-
-    def x_local(k, s):
-        d = piece_dp(k, s)
-        cols = pl.ds(pl.multiple_of((d * n_ctx + ctx) * slab, slab), slab)
-        return pltpu.make_async_copy(
-            xin.at[:, cols], xbuf.at[d, pl.ds(pl.multiple_of(ctx * rows, rows), rows)], xl_sem.at[k, s]
-        )
-
-    pieces = [(k, s) for k in range(nz) for s in range(2)]
 
     def issue(some):
         for k, s in some:
-            if s == 0:
-                x_load(k).wait()
+            for m in range(1, n_ctx):
+                x_pack(k, s, m).wait()
             for j in range(n_ctx - 1):
                 m = 1 + (j + core) % 2 if j < 2 else j + 1
                 x_copy(k, s, m, ctx, peer_to(m)).start()
-            x_local(k, s).start()
 
     issue(pieces[:2])
+    pack(pieces[2:])
 
     length = len_ref[0]
     key_at = lax.broadcasted_iota(jnp.int32, (rows, rows), 0)
@@ -240,8 +244,6 @@
                 copy.wait_recv()
 
     for h in range(group):
-        if h == group // 2:
-            issue(pieces[2:3])
         here = pl.ds(h * rows, rows)
         score = lax.dot_general(kbuf[...], qs[here, :], NT, preferred_element_type=F32) + bias[...]
         top = jnp.max(score, axis=0, keepdims=True)
@@ -274,7 +276,7 @@
         def _():
             grecv[off - 1] = jnp.zeros((rows, 2 * head), BF16)
 
-    issue(pieces[3:4])
+    issue(pieces[2:3])
     gk, gv = kv_grad(reach)
 
     key_t = kbuf[...].astype(F32).T.astype(BF16)
@@ -300,7 +302,7 @@
 
     for o in range(1, n_ctx):
         a_copy(o, ctx, peer_to(o)).start()
-    issue(pieces[4:])
+    issue(pieces[3:])
     for o in range(1, n_ctx):
         a_copy(o, peer_from(o), ctx).wait_recv()
 
@@ -388,7 +390,7 @@
         in_specs=[hbm] * 5 + [vmem, smem],
         out_specs=(vmem, vmem),
         scratch_shapes=[
-            pltpu.VMEM((rows, width), BF16),
+            pltpu.VMEM((n_dp, n_ctx, rows, slab), BF16),
             pltpu.VMEM((keys, head), BF16),
             pltpu.VMEM((keys, head), BF16),
             pltpu.VMEM((group * rows, head), BF16),
@@ -404,7 +406,7 @@
             pltpu.VMEM((nz, 2 * head, slab), BF16),
             pltpu.VMEM((nz - 1, 2 * head, slab), BF16),
             pltpu.VMEM((nz - 1, 2 * head, slab), BF16),
-            dma((nz,)),
+            dma((nz, 2, n_ctx - 1)),
             dma((2 * group + 2,)),
             dma((nz, 2)),
             dma((reach, 2)),

time: 44.1 us -> 43.1 us (0.977)
  the two profiles are of different devices: /device:TPU:29 before, /device:TPU:0 now
where the time goes in v7:
time: 43.1 us; the launch traced here: 42.9 us
  Pallas kernels  41.7 us (97%)
  between operations  1.29 us (3%)
    pallas_call x1, Pallas kernels, fused_shards(): pl.pallas_call(functools.partial(fused_kernel, n_dp, n_ctx, reach), out_s...  39.9 us
    pallas_call x1, Pallas kernels, fused_shards(): pl.pallas_call(hand_over, out_shape=(jax.ShapeDtypeStruct(gq.shape, BF16)...  1.74 us

profile of v7, /device:TPU:0, one launch (start us, length us, event | category | flops | bytes accessed | tf_op | source)
XLA Modules:
  0.0 42.9 jit_solution(16980928393253956225)
XLA Ops:
  1.3 39.9 %shard_map.86 = (bf16[128,1024]{1,0:T(8,128)(2,1)}, bf16[256,256]{1,0:T(8,128)(2,1)}) custom-call(bf16[128,8192]{1,0:T(8,128)(2,1)} %bitcast.6, bf16[128,1024]{1,0:T(8,128)(2,1)} %bitcast.7, bf16[128,128]{1,0:T(8,128)(2,1)} %bitcast.9, bf16[128,128]{1,0:T(8,128)(2,1)} %bitcast.10, bf16[128,1024]{1,0:T(8,128)(2,1)} %bitcast.8, s32[1,512]{1,0:T(1,128)} %seg_ref.1, ...), custom_call_target="tpu_custom_call" | custom-call | tf_op jit(solution)/shard_map/pallas_call | solution.py:384
  41.2 1.7 %shard_map.87 = (bf16[128,1024]{1,0:T(8,128)(2,1)}, bf16[256,256]{1,0:T(8,128)(2,1)}) custom-call(bf16[128,1024]{1,0:T(8,128)(2,1)} %get-tuple-element.6.gq_from, bf16[256,256]{1,0:T(8,128)(2,1)} %get-tuple-element.7.gw_from), custom_call_target="tpu_custom_call" | custom-call | tf_op jit(solution)/shard_map/pallas_call | solution.py:429
